TPU v7x, 128 devices: a whole 4x4x4 slice. The times are simulated.
128 devices in a mesh: tok: 16 (over z_lo, x, core), var: 8 (over z_hi, y).
Axes of the slice: x: 4, y: 4, z: 4 (z_hi: 2, z_lo: 2; z = z_hi * 2 + z_lo), core: 2. Of those that a mesh axis runs over, the one named last changes fastest.
Arguments:
- fields: bfloat16 [48, 6144, 1024], P('var', 'tok'), may hold values from -6 to 6
- var_embed: bfloat16 [48, 1024], replicated, may hold values from -3 to 3
- pos_embed: bfloat16 [6144, 1024], P('tok'), may hold values from -3 to 3
- agg_key: bfloat16 [1024, 1024], replicated, may hold values from -0.1875 to 0.1875
- agg_query: float32 [16, 64], replicated, may hold values from -600 to 600
- agg_value: bfloat16 [1024, 1024], replicated, may hold values from -0.1875 to 0.1875
- agg_out: bfloat16 [1024, 1024], replicated, may hold values from -0.1875 to 0.1875
- gain_one: float32 [1024], replicated, may hold values from 0.1 to 1.9
- qkv_weight: bfloat16 [3, 1024, 1024], P(None, None, 'var'), may hold values from -1 to 1
- attn_out: bfloat16 [1024, 1024], P('var'), may hold values from -0.1875 to 0.1875
- gain_two: float32 [1024], replicated, may hold values from 0.1 to 1.9
- mlp_in: bfloat16 [1024, 4096], P(None, 'var'), may hold values from -0.1875 to 0.1875
- mlp_out: bfloat16 [4096, 1024], P('var'), may hold values from -0.09375 to 0.09375
Outputs:
- encoded: bfloat16 [6144, 1024], P('tok', 'var')
All inputs are finite; a program needn't handle non-finite values.
Results may differ from a plain program's by a relative error of at most 0.029.
Values may be sent and summed in bfloat16 or wider, within the bound.
A program may use at most 128 MiB of HBM per device.

v0:
```python
import math

import jax
import jax.numpy as jnp
from jax import lax
from jax.sharding import PartitionSpec as P

EPS = 1e-05


def layer_norm(stream, gain):
    values = stream.astype(jnp.float32)
    center = values - jnp.mean(values, axis=-1, keepdims=True)
    spread = jnp.mean(center * center, axis=-1, keepdims=True)
    return (center * lax.rsqrt(spread + EPS) * gain).astype(jnp.bfloat16)


def folded_query(agg_key, agg_query):
    width = agg_key.shape[0]
    heads = agg_query.shape[0]
    head_dim = agg_query.shape[1]
    keyed = agg_key.astype(jnp.float32).reshape(width, heads, head_dim)
    folded = jnp.einsum("dhe,he->dh", keyed, agg_query, precision=lax.Precision.HIGHEST)
    return (folded / math.sqrt(head_dim)).astype(jnp.bfloat16)


def weighted_values(embedded, weights, agg_value, heads):
    rows = embedded.shape[1]
    width = embedded.shape[2]

    def weighted_step(total, item):
        field, weight = item
        projected = jnp.dot(field, agg_value, preferred_element_type=jnp.float32).reshape(
            rows, heads, width // heads
        )
        return (total + (weight[:, :, None] * projected).reshape(rows, width), None)

    return lax.scan(weighted_step, jnp.zeros((rows, width), jnp.float32), (embedded, weights))[0]


def grouped_values(embedded, weights, agg_value, heads, groups):
    count = embedded.shape[0]
    rows = embedded.shape[1]
    width = embedded.shape[2]
    per_group = count // groups

    def grouped_step(total, item):
        partial_value = weighted_values(item[0], item[1], agg_value, heads).astype(jnp.bfloat16)
        partial_value = lax.optimization_barrier(partial_value)
        return (total + partial_value.astype(jnp.float32), None)

    blocks = (
        embedded.reshape(groups, per_group, rows, width),
        weights.reshape(groups, per_group, rows, heads),
    )
    return lax.scan(grouped_step, jnp.zeros((rows, width), jnp.float32), blocks)[0]


def body(
    fields,
    var_embed,
    pos_embed,
    agg_key,
    agg_query,
    agg_value,
    agg_out,
    gain_one,
    qkv_weight,
    attn_out,
    gain_two,
    mlp_in,
    mlp_out,
):
    groups = lax.axis_size("var")
    var_index = lax.axis_index("var")
    local_vars = fields.shape[0]
    tok_rows = fields.shape[1]
    width = fields.shape[2]
    heads = agg_query.shape[0]
    head_dim = agg_query.shape[1]
    share = tok_rows // groups
    key_query = folded_query(agg_key, agg_query)
    own_embed = lax.dynamic_slice_in_dim(var_embed, var_index * local_vars, local_vars, 0)
    embedded = (fields.astype(jnp.float32) + own_embed.astype(jnp.float32)[:, None, :]).astype(
        jnp.bfloat16
    )
    spread_rows = embedded.reshape(local_vars, groups, share, width)
    gathered = lax.all_to_all(spread_rows, "var", split_axis=1, concat_axis=0, tiled=True)[:, 0]
    scores = jnp.einsum("vtd,dh->vth", gathered, key_query, preferred_element_type=jnp.float32)
    expd = jnp.exp(scores - jnp.max(scores, axis=0))
    weights = expd / jnp.sum(expd, axis=0)
    mixed_rows = grouped_values(gathered, weights, agg_value, heads, groups).astype(jnp.bfloat16)
    mixed = lax.all_gather(mixed_rows, "var", axis=0, tiled=True)
    stream = (
        jnp.dot(mixed, agg_out, preferred_element_type=jnp.float32) + pos_embed.astype(jnp.float32)
    ).astype(jnp.bfloat16)
    normed = layer_norm(stream, gain_one)
    projected = jnp.einsum(
        "td,kde->kte", normed, qkv_weight, preferred_element_type=jnp.float32
    ).astype(jnp.bfloat16)
    local_heads = projected.shape[2] // head_dim
    head_query = projected[0].reshape(tok_rows, local_heads, head_dim)
    inverse_root = 1.0 / math.sqrt(head_dim)
    start_state = (
        jnp.full((local_heads, tok_rows), -jnp.inf, jnp.float32),
        jnp.zeros((local_heads, tok_rows), jnp.float32),
        jnp.zeros((tok_rows, local_heads, head_dim), jnp.float32),
    )
    key_piece = lax.all_gather(projected[1], "tok", axis=0, tiled=True)
    value_piece = lax.all_gather(projected[2], "tok", axis=0, tiled=True)
    count = key_piece.shape[0]
    shards = max(1, count // tok_rows)
    target = 1 << max(0, (2048 // tok_rows).bit_length() - 1)
    block = math.gcd(shards, target) * tok_rows
    nblocks = count // block
    key_blocks = key_piece.reshape(nblocks, block, local_heads, head_dim)
    value_blocks = value_piece.reshape(nblocks, block, local_heads, head_dim)

    def absorb_step(state, item):
        highest, totals, accum = state
        key_block, value_block = item
        logits = (
            jnp.einsum("qhe,khe->hqk", head_query, key_block, preferred_element_type=jnp.float32)
            * inverse_root
        )
        newest = jnp.maximum(highest, jnp.max(logits, axis=-1))
        rescale = jnp.exp(highest - newest)
        probs = jnp.exp(logits - newest[:, :, None])
        totals = totals * rescale + jnp.sum(probs, axis=-1)
        update = jnp.einsum(
            "hqk,khe->qhe",
            probs.astype(jnp.bfloat16),
            value_block,
            preferred_element_type=jnp.float32,
        )
        accum = accum * rescale.T[:, :, None] + update
        return ((newest, totals, accum), None)

    highest, totals, accum = lax.scan(absorb_step, start_state, (key_blocks, value_blocks))[0]
    attended = (
        (accum / totals.T[:, :, None])
        .reshape(tok_rows, local_heads * head_dim)
        .astype(jnp.bfloat16)
    )
    attn_terms = jnp.dot(attended, attn_out, preferred_element_type=jnp.float32)
    attn_sum = lax.psum(attn_terms.astype(jnp.bfloat16), "var").astype(jnp.float32)
    updated = (stream.astype(jnp.float32) + attn_sum).astype(jnp.bfloat16)
    normed_two = layer_norm(updated, gain_two)
    hidden = jax.nn.gelu(
        jnp.dot(normed_two, mlp_in, preferred_element_type=jnp.float32), approximate=False
    ).astype(jnp.bfloat16)
    down_terms = jnp.dot(hidden, mlp_out, preferred_element_type=jnp.float32)
    mlp_sum = lax.psum_scatter(
        down_terms.astype(jnp.bfloat16), "var", scatter_dimension=1, tiled=True
    ).astype(jnp.float32)
    columns = width // groups
    residual = lax.dynamic_slice_in_dim(updated, var_index * columns, columns, 1)
    return (residual.astype(jnp.float32) + mlp_sum).astype(jnp.bfloat16)


def solution(mesh):
    placed = (
        P("var", "tok", None),
        P(),
        P("tok", None),
        P(),
        P(),
        P(),
        P(),
        P(),
        P(None, None, "var"),
        P("var", None),
        P(),
        P(None, "var"),
        P("var", None),
    )
    return jax.shard_map(
        body, mesh=mesh, in_specs=placed, out_specs=P("tok", "var"), check_vma=False
    )
```

profile of v0, /device:TPU:0, one launch (start us, length us, event | category | flops | bytes accessed | tf_op | source)
XLA Modules:
  0.0 601.4 jit_solution(2328971032060456217)
XLA Ops:
  7.5 3.8 add_convert_fusion
  11.3 3.1 copy.30
  14.3 7.9 %all-to-all-start = ((bf16[6,8,48,1024]{3,2,0,1:T(8,128)(2,1)}), bf16[6,8,48,1024]{3,2,0,1:T(8,128)(2,1)}, u32[]{:S(2)}, u32[]{:S(2)}) async-start(bf16[6,8,48,1024]{3,2,0,1:T(8,128)(2,1)} %copy.30), calls=%async_computation | async-start | bytes 9437184 | tf_op jit(solution)/shard_map/all_to_all | solution.py:88
  22.3 4.0 copy.31
  26.3 4.0 copy.32
  34.0 44.9 %all-to-all-done = bf16[6,8,48,1024]{3,2,0,1:T(8,128)(2,1)} async-done(((bf16[6,8,48,1024]{3,2,0,1:T(8,128)(2,1)}), bf16[6,8,48,1024]{3,2,0,1:T(8,128)(2,1)}, u32[]{:S(2)}, u32[]{:S(2)}) %all-to-all-start) | async-done | bytes 4718624 | tf_op jit(solution)/shard_map/all_to_all | solution.py:88
  78.8 4.7 fusion.131
  84.5 176.3 %while.39 = (s32[]{:T(128)}, f32[48,1024]{1,0:T(8,128)}, bf16[8,6,48,1024]{3,2,1,0:T(8,128)(2,1)}, f32[8,6,48,16]{2,3,1,0:T(8,128)}, bf16[1024,1024]{0,1:T(8,128...) while((s32[]{:T(128)}, f32[48,1024]{1,0:T(8,128)}, bf16[8,6,48,1024]{3,2,1,0:T(8,128)(2,1)}, ...), condition=%wide.region_5.6_spmd.clone, body=%wide.region_2.5_spmd.clone.sunk | while | flops 101007360 | bytes 5785870 | solution.py:56
  86.4 18.6 %while.41 = (s32[]{:T(128)}, f32[48,1024]{1,0:T(8,128)S(1)}, f32[6,48,16]{1,2,0:T(8,128)S(1)}, bf16[6,48,1024]{2,1,0:T(8,128)(2,1)S(1)}, bf16[1024,1024]{0,1:T(8,128)(2,1)}, /*index=5*/s32[]{:T(128)}, s32[]{:T(128)}) while((s32[]{:T(128)}, f32[48,1024]{1,0:T(8,128)S(1)}, f32[6,48,16]{1,2,0:T(8,128)S(1)}, ...), condition=%wide.region_4.4_spmd.clone, body=%wide.region_3.3_spmd.clone.sunk | while | flops 100810752 | bytes 3782751 | solution.py:38
  89.5 2.7 convolution_multiply_fusion.2
  92.6 2.7 convolution_multiply_fusion.2
  95.7 2.7 convolution_multiply_fusion.2
  101.9 2.7 convolution_multiply_fusion.2
  107.6 18.6 %while.41 = (s32[]{:T(128)}, f32[48,1024]{1,0:T(8,128)S(1)}, f32[6,48,16]{1,2,0:T(8,128)S(1)}, bf16[6,48,1024]{2,1,0:T(8,128)(2,1)S(1)}, bf16[1024,1024]{0,1:T(8,128)(2,1)}, /*index=5*/s32[]{:T(128)}, s32[]{:T(128)}) while((s32[]{:T(128)}, f32[48,1024]{1,0:T(8,128)S(1)}, f32[6,48,16]{1,2,0:T(8,128)S(1)}, ...), condition=%wide.region_4.4_spmd.clone, body=%wide.region_3.3_spmd.clone.sunk | while | flops 100810752 | bytes 3782751 | solution.py:38
  110.7 2.7 convolution_multiply_fusion.2
  116.9 2.7 convolution_multiply_fusion.2
  120.0 2.7 convolution_multiply_fusion.2
  123.1 2.7 convolution_multiply_fusion.2
  129.8 18.6 %while.41 = (s32[]{:T(128)}, f32[48,1024]{1,0:T(8,128)S(1)}, f32[6,48,16]{1,2,0:T(8,128)S(1)}, bf16[6,48,1024]{2,1,0:T(8,128)(2,1)S(1)}, bf16[1024,1024]{0,1:T(8,128)(2,1)}, /*index=5*/s32[]{:T(128)}, s32[]{:T(128)}) while((s32[]{:T(128)}, f32[48,1024]{1,0:T(8,128)S(1)}, f32[6,48,16]{1,2,0:T(8,128)S(1)}, ...), condition=%wide.region_4.4_spmd.clone, body=%wide.region_3.3_spmd.clone.sunk | while | flops 100810752 | bytes 3782751 | solution.py:38
  136.0 2.7 convolution_multiply_fusion.2
  142.2 2.7 convolution_multiply_fusion.2
  145.3 2.7 convolution_multiply_fusion.2
  151.9 18.6 %while.41 = (s32[]{:T(128)}, f32[48,1024]{1,0:T(8,128)S(1)}, f32[6,48,16]{1,2,0:T(8,128)S(1)}, bf16[6,48,1024]{2,1,0:T(8,128)(2,1)S(1)}, bf16[1024,1024]{0,1:T(8,128)(2,1)}, /*index=5*/s32[]{:T(128)}, s32[]{:T(128)}) while((s32[]{:T(128)}, f32[48,1024]{1,0:T(8,128)S(1)}, f32[6,48,16]{1,2,0:T(8,128)S(1)}, ...), condition=%wide.region_4.4_spmd.clone, body=%wide.region_3.3_spmd.clone.sunk | while | flops 100810752 | bytes 3782751 | solution.py:38
  155.0 2.7 convolution_multiply_fusion.2
  158.1 2.7 convolution_multiply_fusion.2
  164.3 2.7 convolution_multiply_fusion.2
  174.1 18.6 %while.41 = (s32[]{:T(128)}, f32[48,1024]{1,0:T(8,128)S(1)}, f32[6,48,16]{1,2,0:T(8,128)S(1)}, bf16[6,48,1024]{2,1,0:T(8,128)(2,1)S(1)}, bf16[1024,1024]{0,1:T(8,128)(2,1)}, /*index=5*/s32[]{:T(128)}, s32[]{:T(128)}) while((s32[]{:T(128)}, f32[48,1024]{1,0:T(8,128)S(1)}, f32[6,48,16]{1,2,0:T(8,128)S(1)}, ...), condition=%wide.region_4.4_spmd.clone, body=%wide.region_3.3_spmd.clone.sunk | while | flops 100810752 | bytes 3782751 | solution.py:38
  177.2 2.7 convolution_multiply_fusion.2
  180.3 2.7 convolution_multiply_fusion.2
  186.5 2.7 convolution_multiply_fusion.2
  189.6 2.7 convolution_multiply_fusion.2
  196.2 18.6 %while.41 = (s32[]{:T(128)}, f32[48,1024]{1,0:T(8,128)S(1)}, f32[6,48,16]{1,2,0:T(8,128)S(1)}, bf16[6,48,1024]{2,1,0:T(8,128)(2,1)S(1)}, bf16[1024,1024]{0,1:T(8,128)(2,1)}, /*index=5*/s32[]{:T(128)}, s32[]{:T(128)}) while((s32[]{:T(128)}, f32[48,1024]{1,0:T(8,128)S(1)}, f32[6,48,16]{1,2,0:T(8,128)S(1)}, ...), condition=%wide.region_4.4_spmd.clone, body=%wide.region_3.3_spmd.clone.sunk | while | flops 100810752 | bytes 3782751 | solution.py:38
  199.3 2.7 convolution_multiply_fusion.2
  202.4 2.7 convolution_multiply_fusion.2
  208.6 2.7 convolution_multiply_fusion.2
  218.4 18.6 %while.41 = (s32[]{:T(128)}, f32[48,1024]{1,0:T(8,128)S(1)}, f32[6,48,16]{1,2,0:T(8,128)S(1)}, bf16[6,48,1024]{2,1,0:T(8,128)(2,1)S(1)}, bf16[1024,1024]{0,1:T(8,128)(2,1)}, /*index=5*/s32[]{:T(128)}, s32[]{:T(128)}) while((s32[]{:T(128)}, f32[48,1024]{1,0:T(8,128)S(1)}, f32[6,48,16]{1,2,0:T(8,128)S(1)}, ...), condition=%wide.region_4.4_spmd.clone, body=%wide.region_3.3_spmd.clone.sunk | while | flops 100810752 | bytes 3782751 | solution.py:38
  221.5 2.7 convolution_multiply_fusion.2
  224.6 2.7 convolution_multiply_fusion.2
  227.7 2.7 convolution_multiply_fusion.2
  230.8 2.7 convolution_multiply_fusion.2
  233.9 2.7 convolution_multiply_fusion.2
  240.5 18.6 %while.41 = (s32[]{:T(128)}, f32[48,1024]{1,0:T(8,128)S(1)}, f32[6,48,16]{1,2,0:T(8,128)S(1)}, bf16[6,48,1024]{2,1,0:T(8,128)(2,1)S(1)}, bf16[1024,1024]{0,1:T(8,128)(2,1)}, /*index=5*/s32[]{:T(128)}, s32[]{:T(128)}) while((s32[]{:T(128)}, f32[48,1024]{1,0:T(8,128)S(1)}, f32[6,48,16]{1,2,0:T(8,128)S(1)}, ...), condition=%wide.region_4.4_spmd.clone, body=%wide.region_3.3_spmd.clone.sunk | while | flops 100810752 | bytes 3782751 | solution.py:38
  243.6 2.7 convolution_multiply_fusion.2
  246.7 2.7 convolution_multiply_fusion.2
  252.9 2.7 convolution_multiply_fusion.2
  261.7 48.0 %all_gather.9 = bf16[384,1024]{1,0:T(8,128)(2,1)S(1)} all-gather(bf16[48,1024]{1,0:T(8,128)(2,1)S(1)} %convert_element_type.85), channel_id=1, replica_groups=mesh['tok'=16,'var'=8] {'var'}, dimensions={0}, use_global_device_ids=true | all-gather | bytes 884736 | tf_op jit(solution)/shard_map/all_gather | solution.py:93
  315.0 33.6 %all-gather.5.cloned.1.call-done = bf16[1,6144,128]{1,2,0:T(8,128)(2,1)} async-done(((bf16[1,384,128]{1,2,0:T(8,128)(2,1)}), bf16[1,6144,128]{1,2,0:T(8,128)(2,1)}) %all-gather.5.cloned.1.call-update) | async-done | bytes 1572880 | tf_op jit(solution)/shard_map/all_gather | solution.py:109
  348.6 4.5 reshape.61
  353.1 2.8 copy.34
  356.0 27.6 %all-gather.7.cloned.1.call-done = bf16[1,6144,128]{1,2,0:T(8,128)(2,1)} async-done(((bf16[1,384,128]{1,2,0:T(8,128)(2,1)}), bf16[1,6144,128]{1,2,0:T(8,128)(2,1)}) %all-gather.7.cloned.1.call-update) | async-done | bytes 1572880 | tf_op jit(solution)/shard_map/all_gather | solution.py:110
  383.5 4.6 reshape.62
  388.1 2.8 copy.35
  390.9 34.6 %while.40 = (s32[]{:T(128)}, f32[2,384]{1,0:T(2,128)S(1)}, f32[2,384]{1,0:T(2,128)S(1)}, f32[384,2,64]{0,2,1:T(8,128)S(1)}, bf16[4,1536,2,64]{1,3,2,0:T(8,128)(2...) while((s32[]{:T(128)}, f32[2,384]{1,0:T(2,128)S(1)}, ...), condition=%wide.region_11.12_spmd.clone, body=%wide.region_8.11_spmd.clone.sunk | while | flops 311579136 | bytes 34358404 | solution.py:139
  390.9 4.0 bitcast_reduce_fusion.2
  394.9 3.6 fusion.160
  399.6 3.9 bitcast_reduce_fusion.2
  403.6 3.6 fusion.160
  408.2 3.9 bitcast_reduce_fusion.2
  412.2 3.6 fusion.160
  416.9 3.9 bitcast_reduce_fusion.2
  420.9 3.6 fusion.160
  426.9 86.6 %all-reduce.2.cloned.1.call-done = bf16[384,1024]{1,0:T(8,128)(2,1)} async-done(((bf16[384,1024]{1,0:T(8,128)(2,1)}), bf16[384,1024]{1,0:T(8,128)(2,1)}) %all-reduce.2.cloned.1.call-update) | async-done | bytes 786448 | tf_op jit(solution)/shard_map/psum | solution.py:146
  515.6 5.2 convolution_convert_fusion
  523.1 70.1 %reduce-scatter.4.cloned.1.call-done = bf16[128,384]{1,0:T(8,128)(2,1)} async-done(((bf16[1024,384]{1,0:T(8,128)(2,1)}), bf16[128,384]{1,0:T(8,128)(2,1)}) %reduce-scatter.4.cloned.1.call-update) | async-done | bytes 98320
  (325 shorter events, 119.0 us)
Async XLA Ops:
  6.5 303.2 %copy-start = (bf16[1024,1024]{1,0:T(8,128)(2,1)S(1)}, bf16[1024,1024]{1,0:T(8,128)(2,1)}, u32[]{:S(2)}) copy-start(bf16[1024,1024]{1,0:T(8,128)(2,1)} %param.25) | copy-start | bytes 6291460
  14.3 64.5 %all-to-all-start = ((bf16[6,8,48,1024]{3,2,0,1:T(8,128)(2,1)}), bf16[6,8,48,1024]{3,2,0,1:T(8,128)(2,1)}, u32[]{:S(2)}, u32[]{:S(2)}) async-start(bf16[6,8,48,1024]{3,2,0,1:T(8,128)(2,1)} %copy.30), calls=%async_computation | async-start | bytes 9437184 | tf_op jit(solution)/shard_map/all_to_all | solution.py:88
  22.2 326.4 %all-gather.5.cloned.1.call-start = ((), (), s32[]{:S(2)}) async-start(), calls=%async_computation.3 | async-start | bytes 1671168 | tf_op jit(solution)/shard_map/all_gather | solution.py:109
  26.3 4.0 copy-start.3
  26.3 5.2 copy-start.6
  309.7 2.7 copy-start.4
  309.7 2.7 copy-start.7
  312.0 1.2 copy-start.2
  314.0 69.6 %all-gather.7.cloned.1.call-start = ((), (), s32[]{:S(2)}) async-start(), calls=%async_computation.4 | async-start | bytes 1671168 | tf_op jit(solution)/shard_map/all_gather | solution.py:110
  314.7 198.8 %all-reduce.2.cloned.1.call-start = ((), (), s32[]{:S(2)}) async-start(), calls=%async_computation.2 | async-start | bytes 1572864 | tf_op jit(solution)/shard_map/psum | solution.py:146
  390.9 34.6 %copy-start.5 = (bf16[128,1024]{1,0:T(8,128)(2,1)S(1)}, bf16[128,1024]{1,0:T(8,128)(2,1)}, u32[]{:S(2)}) copy-start(bf16[128,1024]{1,0:T(8,128)(2,1)} %param.28) | copy-start | bytes 786436
  394.9 3.9 copy-start.1
  403.6 3.9 copy-start.1
  412.2 3.9 copy-start.1
  420.8 3.9 copy-start.1
  426.9 88.7 %copy-start.8 = (f32[1024]{0:T(1024)S(1)}, f32[1024]{0:T(1024)}, u32[]{:S(2)}) copy-start(f32[1024]{0:T(1024)} %param.29) | copy-start | bytes 12292
  426.9 166.3 %reduce-scatter.4.cloned.1.call-start = ((), (), s32[]{:S(2)}) async-start(), calls=%async_computation.5 | async-start | bytes 884736
Sparse Core Ops, SparseCore 0:
  314.1 34.4 all-gather.4
  350.2 33.2 all-gather.6
  427.0 86.4 all-reduce.1
  523.2 69.9 reduce-scatter.3
where the time goes:
time: 605 us; the launch traced here: 601 us
  waiting for transfers between devices  264 us (44%)
  matrix products  176 us (29%)
  local copies, waits for them, and re-layouts  61.3 us (10%)
  blocking collectives  48 us (8%)
  other arithmetic  28.2 us (5%)
  between operations  13.3 us (2%)
  starting transfers between devices  8.2 us (1%)
    dot_general x48, matrix products, weighted_step(): jnp.dot(field, agg_value, preferred_element_type=jnp.float32)  130 us
    psum x1, waiting for transfers between devices, body(): lax.psum(attn_terms.astype(jnp.bfloat16), 'var').astype(jnp.float32)  86.6 us
    unnamed x5, waiting for transfers between devices  70.9 us
    all_gather x1, blocking collectives, body(): mixed = lax.all_gather(mixed_rows, 'var', axis=0, tiled=True)  48 us
    all_to_all x1, waiting for transfers between devices, body(): lax.all_to_all(spread_rows, 'var', split_axis=1, concat_axis=0, tiled=True)  44.9 us
    all_gather x1, waiting for transfers between devices, body(): key_piece = lax.all_gather(projected[1], 'tok', axis=0, tiled=True)  33.6 us
    all_gather x1, waiting for transfers between devices, body(): value_piece = lax.all_gather(projected[2], 'tok', axis=0, tiled=True)  27.6 us
    unnamed x23, local copies, waits for them, and re-layouts  18.2 us
  transfers between devices with their start and end apart: 5, of which 5 were waited for; matrix products, arithmetic and copies ran while one was open for 3% of the time, Pallas kernels for 0%

commit v1 on v0

v1 whole, which is shorter than its diff:
```python
import functools

import jax
import jax.numpy as jnp
from jax import lax
from jax.experimental import pallas as pl
from jax.experimental.pallas import tpu as pltpu
from jax.sharding import PartitionSpec as P

EPS = 1e-05
MESH = pl.DeviceIdType.MESH
BF = jnp.bfloat16
F32 = jnp.float32
GROUPS = 8
SHARE = 48
ROWS = 384
WIDTH = 1024
LANES = 128
LOCAL_VARS = 6
LOADS = 12


def mm(a, b):
    return jnp.dot(a, b, preferred_element_type=F32)


def mm_nt(a, b):
    return lax.dot_general(a, b, (((1,), (1,)), ((), ())), preferred_element_type=F32)


def lane_of(shape):
    return lax.broadcasted_iota(jnp.int32, shape, len(shape) - 1)


def split_three(value):
    high = value.astype(BF).astype(F32)
    rest = value - high
    middle = rest.astype(BF).astype(F32)
    return high, middle, rest - middle


def layer_norm(values, gain):
    center = values - jnp.mean(values, axis=-1, keepdims=True)
    spread = jnp.mean(center * center, axis=-1, keepdims=True)
    return (center * lax.rsqrt(spread + EPS) * gain).astype(BF)


def kernel(
    fields,
    var_embed,
    pos_embed,
    agg_key,
    agg_query,
    agg_value,
    agg_out,
    gain_one,
    qkv_weight,
    attn_out,
    gain_two,
    mlp_in,
    mlp_out,
    out,
    field_s,
    embed_s,
    pos_s,
    key_s,
    query_s,
    value_s,
    aggout_s,
    gain1_s,
    qkv_s,
    attnout_s,
    gain2_s,
    mlpin_s,
    mlpout_s,
    kq_s,
    spread_s,
    pick_s,
    emb_s,
    part_s,
    part_r,
    norm_r,
    q_s,
    qout_s,
    qin_r,
    kvout_s,
    kv_r,
    max_s,
    acc_s,
    att_s,
    att_r,
    upd_r,
    down_s,
    down_r,
    load_sem,
    field_sem,
    p1_send,
    p1_recv,
    p3_send,
    p3_recv,
    z_send,
    z_recv,
    kv_send,
    kv_recv,
    w_send,
    w_recv,
    a_send,
    a_recv,
    p8_send,
    p8_recv,
    p10_send,
    p10_recv,
):
    tok = lax.axis_index("tok")
    me = lax.axis_index("var")
    core = lax.rem(tok, 2)
    half = tok // 8
    ring = lax.rem(tok // 2, 4)
    sibling = tok + 1 - 2 * core
    partner = tok + 8 - 16 * half

    def along_x(step):
        return half * 8 + lax.rem(ring + step, 4) * 2 + core

    def peer(step):
        return lax.rem(me + 1 + step, GROUPS)

    def remote(src, dst, send, recv, to_tok, to_var):
        return pltpu.make_async_remote_copy(
            src_ref=src,
            dst_ref=dst,
            send_sem=send,
            recv_sem=recv,
            device_id=(to_tok, to_var),
            device_id_type=MESH,
        )

    barrier = pltpu.get_barrier_semaphore()
    others = [(tok, peer(i)) for i in range(GROUPS - 1)]
    others += [(partner, lax.rem(me + i, GROUPS)) for i in range(GROUPS)]
    others += [(sibling, me)] + [(along_x(i), me) for i in (1, 2, 3)]
    for device in others:
        pl.semaphore_signal(barrier, inc=1, device_id=device, device_id_type=MESH)

    def field_copy(i):
        rows = pl.ds(pl.multiple_of(peer(i) * SHARE, 16), SHARE)
        return pltpu.make_async_copy(fields.at[:, rows, :], field_s.at[i], field_sem.at[i])

    own_rows = pl.ds(pl.multiple_of(me * SHARE, 16), SHARE)
    loads = [
        pltpu.make_async_copy(src, dst, load_sem.at[k])
        for k, (src, dst) in enumerate(
            [
                (agg_query, query_s),
                (var_embed, embed_s),
                (agg_key, key_s),
                (agg_value, value_s),
                (agg_out, aggout_s),
                (pos_embed.at[own_rows, :], pos_s),
                (gain_one, gain1_s),
                (qkv_weight, qkv_s),
                (attn_out, attnout_s.at[me]),
                (gain_two, gain2_s),
                (mlp_in, mlpin_s),
                (mlp_out, mlpout_s),
            ]
        )
    ]
    for k in range(3):
        loads[k].start()
    field_copy(0).start()
    loads[3].start()
    for i in range(1, GROUPS):
        field_copy(i).start()
    for k in range(4, LOADS):
        loads[k].start()

    row = lax.broadcasted_iota(jnp.int32, (LANES, WIDTH), 0)
    col = lax.broadcasted_iota(jnp.int32, (LANES, WIDTH), 1)
    spread_s[...] = jnp.where((row < 32) & (row % 16 == col // 64), 1.0, 0.0).astype(BF)
    row = lax.broadcasted_iota(jnp.int32, (LANES, LANES), 0)
    col = lax.broadcasted_iota(jnp.int32, (LANES, LANES), 1)
    same = row % 16 == col % 16
    pick_s[0] = jnp.where(same & (row < 48), 1.0, 0.0).astype(BF)
    pick_s[1] = jnp.where(same & (row >= 48) & (row < 96), 1.0, 0.0).astype(BF)

    loads[0].wait()
    heads = query_s[...]
    tiled = jnp.concatenate([heads] * 16, axis=1)
    row = lax.broadcasted_iota(jnp.int32, (16, WIDTH), 0)
    col = lax.broadcasted_iota(jnp.int32, (16, WIDTH), 1)
    tiled = jnp.where(col // 64 == row, tiled, 0.0)
    stacked = jnp.concatenate(split_three(tiled), axis=0).astype(BF)
    loads[2].wait()
    folded = mm_nt(stacked, key_s[...])
    folded = ((folded[0:16] + folded[16:32] + folded[32:48]) * 0.125).astype(BF)
    kq_s[...] = jnp.concatenate([folded] * 8, axis=0)

    loads[1].wait()
    row = lax.broadcasted_iota(jnp.int32, (16, 48), 0)
    col = lax.broadcasted_iota(jnp.int32, (16, 48), 1)
    chosen = jnp.where((col == me * LOCAL_VARS + row) & (row < LOCAL_VARS), 1.0, 0.0).astype(BF)
    own_embed = mm(chosen, embed_s[...]).astype(BF)
    loads[3].wait()
    pl.semaphore_wait(barrier, len(others))

    lane = lane_of((SHARE, LANES))

    def aggregate_step(i, carry):
        field_copy(i).wait()
        for v in range(LOCAL_VARS):
            emb_s[v * SHARE : (v + 1) * SHARE, :] = field_s[i, v] + own_embed[v : v + 1, :]
        scores = mm_nt(emb_s[...], kq_s[...]).reshape(LOCAL_VARS, SHARE, LANES)
        highest = jnp.max(scores, axis=0)
        expd = jnp.exp(scores - highest[None])
        totals = jnp.sum(expd, axis=0)
        coarse = expd.astype(BF).astype(F32)
        weights = jnp.where((lane < 16)[None], coarse, jnp.where((lane < 32)[None], expd - coarse, 0.0))
        weights = weights.reshape(LOCAL_VARS * SHARE, LANES).astype(BF)
        for n in range(4):
            cols = slice(n * 256, (n + 1) * 256)
            wide = mm(weights, spread_s[:, cols])
            projected = mm(emb_s[...], value_s[:, cols])
            term = (wide * projected).reshape(LOCAL_VARS, SHARE, 256)
            part_s[i, :, cols] = jnp.sum(term, axis=0).astype(BF)
        high, middle, low = split_three(highest)
        high_t, middle_t, low_t = split_three(totals)
        notes = jnp.where(lane < 16, high, jnp.where(lane < 32, middle, low))
        notes_t = jnp.where(lane < 64, high_t, jnp.where(lane < 80, middle_t, low_t))
        part_s[i, :, WIDTH:] = jnp.where(lane < 48, notes, notes_t).astype(BF)

        @pl.when(i < GROUPS - 1)
        def _():
            remote(
                part_s.at[i], part_r.at[me], p1_send.at[i], p1_recv.at[me], tok, peer(i)
            ).start()

        return carry

    lax.fori_loop(0, GROUPS, aggregate_step, 0)
    part_r[me] = part_s[GROUPS - 1]

    def p1_copy(i):
        return remote(
            part_s.at[i], part_r.at[peer(i)], p1_send.at[i], p1_recv.at[peer(i)], tok, peer(i)
        )

    for i in range(GROUPS - 1):
        p1_copy(i).wait_recv()

    notes = part_r[:, :, WIDTH:].reshape(ROWS, LANES)
    highest = mm(notes, pick_s[0]).reshape(GROUPS, SHARE, LANES)
    totals = mm(notes, pick_s[1]).reshape(GROUPS, SHARE, LANES)
    scale = jnp.exp(highest - jnp.max(highest, axis=0)[None])
    scale = scale / jnp.sum(scale * totals, axis=0)[None]
    coarse = scale.astype(BF).astype(F32)
    scale = jnp.where((lane < 16)[None], coarse, jnp.where((lane < 32)[None], scale - coarse, 0.0))
    scale = scale.reshape(ROWS, LANES).astype(BF)
    mixed = []
    for n in range(4):
        cols = slice(n * 256, (n + 1) * 256)
        wide = mm(scale, spread_s[:, cols]).reshape(GROUPS, SHARE, 256)
        mixed.append(jnp.sum(wide * part_r[:, :, cols].astype(F32), axis=0).astype(BF))
    mixed = jnp.concatenate(mixed, axis=1)
    for k in (4, 5, 6):
        loads[k].wait()
    stream = (mm(mixed, aggout_s[...]) + pos_s[...].astype(F32)).astype(BF)
    norm_r[me] = layer_norm(stream.astype(F32), gain1_s[...])

    def gather_copy(buffer, send, recv, i, source):
        return remote(buffer.at[source], buffer.at[source], send.at[i], recv.at[source], tok, peer(i))

    for i in range(GROUPS - 1):
        gather_copy(norm_r, p3_send, p3_recv, i, me).start()
    loads[7].wait()
    loads[8].wait()
    for i in range(GROUPS - 1):
        gather_copy(norm_r, p3_send, p3_recv, i, peer(i)).wait_recv()

    normed = norm_r[...].reshape(ROWS, WIDTH)
    keys = mm(normed, qkv_s[1])
    values = mm(normed, qkv_s[2])
    wide_lane = lane_of((ROWS, LANES))
    left = wide_lane < 64
    kv_a = jnp.where(left, keys, pltpu.roll(values, 64, 1)).astype(BF)
    kv_b = jnp.where(left, pltpu.roll(keys, 64, 1), values).astype(BF)
    first = half == 0
    kv_r[core] = jnp.where(first, kv_a, kv_b)
    kvout_s[...] = jnp.where(first, kv_b, kv_a)

    def slot(order, owner):
        return order * 2 + owner

    z_kv = remote(kvout_s, kv_r.at[slot(1, core)], z_send.at[0], kv_recv.at[slot(1, core)], partner, me)
    z_kv.start()
    hops = ((2, 3), (3, 1), (4, 2))

    def x_copy(k, order, source):
        to = slot(order, core)
        return remote(
            kv_r.at[source], kv_r.at[to], kv_send.at[k], kv_recv.at[to], along_x(hops[k % 3][1]), me
        )

    for k in range(3):
        x_copy(k, hops[k][0], slot(0, core)).start()

    def share_copy(order, owner):
        at = slot(order, owner)
        return remote(kv_r.at[at], kv_r.at[at], kv_send.at[8 + order], kv_recv.at[at], sibling, me)

    share_copy(0, core).start()
    queries = mm(normed, qkv_s[0]) * 0.125
    rolled = pltpu.roll(queries, 64, 1)
    q_a = jnp.where(left, queries, 0.0).astype(BF)
    q_b = jnp.where(left, rolled, 0.0).astype(BF)
    q_s[0:ROWS, :] = jnp.where(first, q_a, q_b)
    other = jnp.where(first, rolled, queries)
    qout_s[...] = jnp.where(
        left[: ROWS // 2], other[: ROWS // 2], pltpu.roll(other[ROWS // 2 :], 64, 1)
    ).astype(BF)
    z_q = remote(qout_s, qin_r, z_send.at[1], z_recv.at[0], partner, me)
    z_q.start()

    w_rows = pl.ds(pl.multiple_of(core * 64, 64), 64)

    def w_copy(i, source):
        at = attnout_s.at[source, w_rows, :]
        return remote(at, at, w_send.at[i], w_recv.at[source], tok, peer(i))

    for i in range(GROUPS - 1):
        w_copy(i, me).start()

    max_s[...] = jnp.full(max_s.shape, -jnp.inf, F32)
    acc_s[...] = jnp.zeros(acc_s.shape, F32)
    z_kv.wait_recv()
    for k in range(3):
        x_copy(3 + k, hops[k][0] + 3, slot(1, core)).start()
    z_q.wait_recv()
    packed = qin_r[...].astype(F32)
    q_s[ROWS : ROWS + ROWS // 2, :] = jnp.where(left[: ROWS // 2], packed, 0.0).astype(BF)
    q_s[ROWS + ROWS // 2 :, :] = jnp.where(
        left[: ROWS // 2], pltpu.roll(packed, 64, 1), 0.0
    ).astype(BF)

    def absorb(at):
        block = kv_r[at]
        ones = jnp.where(left, 1.0, block.astype(F32)).astype(BF)
        for n in range(3):
            rows = slice(n * 256, (n + 1) * 256)
            logits = mm_nt(q_s[rows, :], block)
            before = max_s[rows, :]
            newest = jnp.maximum(before, jnp.max(logits, axis=1, keepdims=True))
            probs = jnp.exp(logits - jnp.concatenate([newest] * 3, axis=1)).astype(BF)
            acc_s[rows, :] = acc_s[rows, :] * jnp.exp(before - newest) + mm(probs, ones)
            max_s[rows, :] = newest

    def attend_step(order, carry):
        own = slot(order, core)
        theirs = slot(order, 1 - core)

        @pl.when(order > 1)
        def _():
            remote(kv_r.at[own], kv_r.at[own], kv_send.at[0], kv_recv.at[own], sibling, me).wait_recv()

        @pl.when(order > 0)
        def _():
            share_copy(order, core).start()

        absorb(own)
        share_copy(order, 1 - core).wait_recv()
        absorb(theirs)
        return carry

    lax.fori_loop(0, 8, attend_step, 0)

    acc = acc_s[...]
    turned = pltpu.roll(acc, 64, 1)
    wide_left = lane_of((2 * ROWS, LANES)) < 64
    result = jnp.where(wide_left, turned, acc) / jnp.where(wide_left, acc, turned)
    keep = wide_left == jnp.broadcast_to(first, wide_left.shape)
    att_s[...] = jnp.where(keep, result, 0.0).astype(BF).reshape(2, GROUPS, SHARE, LANES)
    att_r[half, me] = att_s[0, me]

    def att_copy(side, i, at, source):
        to = lax.rem(me + 1 + i, GROUPS)
        return remote(
            att_s.at[side, to],
            att_r.at[at, source],
            a_send.at[side * GROUPS + i],
            a_recv.at[at * GROUPS + source],
            tok if side == 0 else partner,
            to,
        )

    for i in range(GROUPS - 1):
        att_copy(0, i, half, me).start()
        att_copy(1, i, half, me).start()
    att_copy(1, GROUPS - 1, half, me).start()

    def w_share(i, rows):
        at = attnout_s.at[peer(i), rows, :]
        return remote(at, at, w_send.at[GROUPS + i], w_recv.at[GROUPS + peer(i)], sibling, me)

    their_rows = pl.ds(pl.multiple_of(64 - core * 64, 64), 64)
    for i in range(GROUPS - 1):
        w_copy(i, peer(i)).wait_recv()
        w_share(i, w_rows).start()
    for i in range(GROUPS - 1):
        w_share(i, their_rows).wait_recv()
    for i in range(GROUPS - 1):
        att_copy(0, i, half, peer(i)).wait_recv()
    for i in range(GROUPS):
        att_copy(1, i, 1 - half, peer(i)).wait_recv()

    attended = jnp.concatenate([att_r[0, g] + att_r[1, g] for g in range(GROUPS)], axis=1)
    attn_sum = mm(attended, attnout_s[...].reshape(WIDTH, WIDTH))
    upd_r[me] = (stream.astype(F32) + attn_sum).astype(BF)
    for i in range(GROUPS - 1):
        gather_copy(upd_r, p8_send, p8_recv, i, me).start()
    for k in (9, 10, 11):
        loads[k].wait()
    for i in range(GROUPS - 1):
        gather_copy(upd_r, p8_send, p8_recv, i, peer(i)).wait_recv()

    updated = upd_r[...].reshape(ROWS, WIDTH)
    normed_two = layer_norm(updated.astype(F32), gain2_s[...])
    raised = mm(normed_two, mlpin_s[...])
    hidden = (0.5 * raised * (1.0 + lax.erf(raised * 0.7071067811865476))).astype(BF)
    for n in range(4):
        terms = mm(hidden, mlpout_s[:, n * 256 : (n + 1) * 256]).astype(BF)
        down_s[2 * n] = terms[:, :LANES]
        down_s[2 * n + 1] = terms[:, LANES:]

    def down_copy(i, source):
        return remote(
            down_s.at[peer(i)],
            down_r.at[source],
            p10_send.at[i],
            p10_recv.at[source],
            tok,
            peer(i),
        )

    for i in range(GROUPS - 1):
        down_copy(i, me).start()
    total = down_s[me].astype(F32)
    own_cols = pl.ds(pl.multiple_of(me * LANES, LANES), LANES)
    residual = upd_r[:, :, own_cols].reshape(ROWS, LANES).astype(F32)
    for i in range(GROUPS - 1):
        down_copy(i, peer(i)).wait_recv()
        total = total + down_r[peer(i)].astype(F32)
    out[...] = (residual + total).astype(BF)

    for i in range(GROUPS - 1):
        p1_copy(i).wait_send()
        gather_copy(norm_r, p3_send, p3_recv, i, me).wait_send()
        w_copy(i, me).wait_send()
        w_share(i, w_rows).wait_send()
        att_copy(0, i, half, me).wait_send()
        gather_copy(upd_r, p8_send, p8_recv, i, me).wait_send()
        down_copy(i, me).wait_send()
    for i in range(GROUPS):
        att_copy(1, i, half, me).wait_send()
        share_copy(i, core).wait_send()
    for k in range(3):
        x_copy(k, hops[k][0], slot(0, core)).wait_send()
        x_copy(3 + k, hops[k][0] + 3, slot(1, core)).wait_send()
    z_kv.wait_send()
    z_q.wait_send()


def scratch():
    vmem = pltpu.VMEM
    dma = pltpu.SemaphoreType.DMA
    return [
        vmem((GROUPS, LOCAL_VARS, SHARE, WIDTH), BF),
        vmem((48, WIDTH), BF),
        vmem((SHARE, WIDTH), BF),
        vmem((WIDTH, WIDTH), BF),
        vmem((16, 64), F32),
        vmem((WIDTH, WIDTH), BF),
        vmem((WIDTH, WIDTH), BF),
        vmem((1, WIDTH), F32),
        vmem((3, WIDTH, LANES), BF),
        vmem((GROUPS, LANES, WIDTH), BF),
        vmem((1, WIDTH), F32),
        vmem((WIDTH, 512), BF),
        vmem((512, WIDTH), BF),
        vmem((LANES, WIDTH), BF),
        vmem((LANES, WIDTH), BF),
        vmem((2, LANES, LANES), BF),
        vmem((LOCAL_VARS * SHARE, WIDTH), BF),
        vmem((GROUPS, SHARE, WIDTH + LANES), BF),
        vmem((GROUPS, SHARE, WIDTH + LANES), BF),
        vmem((GROUPS, SHARE, WIDTH), BF),
        vmem((2 * ROWS, LANES), BF),
        vmem((ROWS // 2, LANES), BF),
        vmem((ROWS // 2, LANES), BF),
        vmem((ROWS, LANES), BF),
        vmem((16, ROWS, LANES), BF),
        vmem((2 * ROWS, LANES), F32),
        vmem((2 * ROWS, LANES), F32),
        vmem((2, GROUPS, SHARE, LANES), BF),
        vmem((2, GROUPS, SHARE, LANES), BF),
        vmem((GROUPS, SHARE, WIDTH), BF),
        vmem((GROUPS, ROWS, LANES), BF),
        vmem((GROUPS, ROWS, LANES), BF),
        dma((LOADS,)),
        dma((GROUPS,)),
        dma((GROUPS,)),
        dma((GROUPS,)),
        dma((GROUPS,)),
        dma((GROUPS,)),
        dma((2,)),
        dma((1,)),
        dma((16,)),
        dma((16,)),
        dma((2 * GROUPS,)),
        dma((2 * GROUPS,)),
        dma((2 * GROUPS,)),
        dma((2 * GROUPS,)),
        dma((GROUPS,)),
        dma((GROUPS,)),
        dma((GROUPS,)),
        dma((GROUPS,)),
    ]


def body(
    fields,
    var_embed,
    pos_embed,
    agg_key,
    agg_query,
    agg_value,
    agg_out,
    gain_one,
    qkv_weight,
    attn_out,
    gain_two,
    mlp_in,
    mlp_out,
):
    return pl.pallas_call(
        kernel,
        out_shape=jax.ShapeDtypeStruct((ROWS, LANES), BF),
        in_specs=[pl.BlockSpec(memory_space=pl.ANY)] * 13,
        out_specs=pl.BlockSpec(memory_space=pltpu.VMEM),
        scratch_shapes=scratch(),
        compiler_params=pltpu.CompilerParams(
            collective_id=0, has_side_effects=True, vmem_limit_bytes=56 * 2**20
        ),
    )(
        fields,
        var_embed,
        pos_embed,
        agg_key,
        agg_query,
        agg_value,
        agg_out,
        gain_one.reshape(1, WIDTH),
        qkv_weight,
        attn_out,
        gain_two.reshape(1, WIDTH),
        mlp_in,
        mlp_out,
    )


def solution(mesh):
    placed = (
        P("var", "tok", None),
        P(),
        P("tok", None),
        P(),
        P(),
        P(),
        P(),
        P(),
        P(None, None, "var"),
        P("var", None),
        P(),
        P(None, "var"),
        P("var", None),
    )
    return jax.shard_map(
        body, mesh=mesh, in_specs=placed, out_specs=P("tok", "var"), check_vma=False
    )
```

time: 605 us -> 101 us (0.17)
  waiting for transfers between devices: 264 us -> 0 us
  matrix products: 176 us -> 0 us
  Pallas kernels: 0 us -> 99.2 us
  local copies, waits for them, and re-layouts: 61.3 us -> 1.54 us
  blocking collectives: 48 us -> 0 us
  other arithmetic: 28.2 us -> 0 us
  between operations: 13.3 us -> 0.01 us
  starting transfers between devices: 8.2 us -> 0 us
    dot_general x61 -> x0, matrix products: 176 us -> none  [the longest x48 130 us: weighted_step(): jnp.dot(field, agg_value, preferred_element_type=jnp.float32)]
    pallas_call x0 -> x1, Pallas kernels: none -> 99.2 us  [body(): pl.pallas_call(kernel, out_shape=jax.ShapeDtypeStruct((ROWS, LANES), BF),...]
    psum x1 -> x0, waiting for transfers between devices: 86.6 us -> none  [body(): lax.psum(attn_terms.astype(jnp.bfloat16), 'var').astype(jnp.float32)]
    unnamed x5 -> x0, waiting for transfers between devices: 70.9 us -> none
    all_gather x2 -> x0, waiting for transfers between devices: 61.2 us -> none  [the longest x1 33.6 us: body(): key_piece = lax.all_gather(projected[1], 'tok', axis=0, tiled=True)]
    all_gather x1 -> x0, blocking collectives: 48 us -> none  [body(): mixed = lax.all_gather(mixed_rows, 'var', axis=0, tiled=True)]
    all_to_all x1 -> x0, waiting for transfers between devices: 44.9 us -> none  [body(): lax.all_to_all(spread_rows, 'var', split_axis=1, concat_axis=0, tiled=True)]
    reshape x51 -> x0, local copies, waits for them, and re-layouts: 19.5 us -> none  [the longest x48 7.3 us: weighted_step(): return (total + (weight[:, :, None] * projected).reshape(rows, width), None)]
  transfers between devices with their start and end apart: 5 -> 0, of which waited for: 5 -> 0; matrix products, arithmetic and copies ran while one was open for 3% -> 0% of each run, Pallas kernels for 0% -> 0%
where the time goes in v1:
time: 101 us
  Pallas kernels  99.2 us (98%)
  local copies, waits for them, and re-layouts  1.54 us (2%)
    pallas_call x1, Pallas kernels, body(): pl.pallas_call(kernel, out_shape=jax.ShapeDtypeStruct((ROWS, LANES), BF),...  99.2 us

profile of v1, /device:TPU:0, one launch (start us, length us, event | category | flops | bytes accessed | tf_op | source)
XLA Modules:
  0.0 100.7 jit_solution(1207700971897993669)
XLA Ops:
  0.0 99.2 %shard_map.127 = bf16[384,128]{1,0:T(8,128)(2,1)} custom-call(bf16[6,384,1024]{2,1,0:T(8,128)(2,1)} %fields.1, bf16[48,1024]{1,0:T(8,128)(2,1)} %var_embed.1, bf16[384,1024]{1,0:T(8,128)(2,1)} %pos_embed.1, bf16[1024,1024]{1,0:T(8,128)(2,1)} %agg_key.1, f32[16,64]{1,0:T(8,128)} %agg_query.1, bf16[1024,1024]{1,0:T(8,128)(2,1)} %agg_value.1, ...), custom_call_target="tpu_custom_call" | custom-call | tf_op jit(solution)/shard_map/pallas_call | solution.py:544
  99.2 1.5 %copy.15 = bf16[384,128]{1,0:T(8,128)(2,1)} copy(bf16[384,128]{1,0:T(8,128)(2,1)} %shard_map.127) | data formatting | bytes 196608

commit v2 on v1

--- a/solution.py
+++ b/solution.py
@@ -77,6 +77,7 @@
     spread_s,
     pick_s,
     emb_s,
+    weight_s,
     part_s,
     part_r,
     norm_r,
@@ -90,6 +91,7 @@
     att_s,
     att_r,
     upd_r,
+    res_r,
     down_s,
     down_r,
     load_sem,
@@ -104,6 +106,8 @@
     kv_recv,
     w_send,
     w_recv,
+    v_send,
+    v_recv,
     a_send,
     a_recv,
     p8_send,
@@ -122,8 +126,11 @@
     def along_x(step):
         return half * 8 + lax.rem(ring + step, 4) * 2 + core
 
+    plane = me // 4
+    high_y = lax.rem(me, 4)
+
     def peer(step):
-        return lax.rem(me + 1 + step, GROUPS)
+        return lax.rem(plane + 1 + step // 4, 2) * 4 + lax.rem(high_y + 3 - step % 4, 4)
 
     def remote(src, dst, send, recv, to_tok, to_var):
         return pltpu.make_async_remote_copy(
@@ -159,21 +166,18 @@
                 (pos_embed.at[own_rows, :], pos_s),
                 (gain_one, gain1_s),
                 (qkv_weight, qkv_s),
-                (attn_out, attnout_s.at[me]),
+                (attn_out.at[ring, core], attnout_s.at[me, ring, core]),
                 (gain_two, gain2_s),
-                (mlp_in, mlpin_s),
-                (mlp_out, mlpout_s),
+                (mlp_in, mlpin_s.at[0]),
+                (mlp_out, mlpout_s.at[0]),
             ]
         )
     ]
-    for k in range(3):
+    for k in (8, 0, 1, 2):
         loads[k].start()
     field_copy(0).start()
     loads[3].start()
-    for i in range(1, GROUPS):
-        field_copy(i).start()
-    for k in range(4, LOADS):
-        loads[k].start()
+    field_copy(1).start()
 
     row = lax.broadcasted_iota(jnp.int32, (LANES, WIDTH), 0)
     col = lax.broadcasted_iota(jnp.int32, (LANES, WIDTH), 1)
@@ -190,63 +194,108 @@
     row = lax.broadcasted_iota(jnp.int32, (16, WIDTH), 0)
     col = lax.broadcasted_iota(jnp.int32, (16, WIDTH), 1)
     tiled = jnp.where(col // 64 == row, tiled, 0.0)
-    stacked = jnp.concatenate(split_three(tiled), axis=0).astype(BF)
+    stacked = jnp.concatenate(split_three(tiled) + (jnp.zeros((80, WIDTH), F32),), axis=0)
+    stacked = stacked.T.astype(BF)
     loads[2].wait()
-    folded = mm_nt(stacked, key_s[...])
-    folded = ((folded[0:16] + folded[16:32] + folded[32:48]) * 0.125).astype(BF)
-    kq_s[...] = jnp.concatenate([folded] * 8, axis=0)
+    folded = mm(key_s[...], stacked)
+    folded = folded + pltpu.roll(folded, 112, 1) + pltpu.roll(folded, 96, 1)
+    folded = jnp.where(lane_of((WIDTH, LANES)) < 16, folded * 0.125, 0.0)
+    for shift in (16, 32, 64):
+        folded = folded + pltpu.roll(folded, shift, 1)
+    kq_s[...] = folded.astype(BF)
 
     loads[1].wait()
     row = lax.broadcasted_iota(jnp.int32, (16, 48), 0)
     col = lax.broadcasted_iota(jnp.int32, (16, 48), 1)
     chosen = jnp.where((col == me * LOCAL_VARS + row) & (row < LOCAL_VARS), 1.0, 0.0).astype(BF)
     own_embed = mm(chosen, embed_s[...]).astype(BF)
-    loads[3].wait()
-    pl.semaphore_wait(barrier, len(others))
+
+    across = lax.rem(me + 4, GROUPS)
+    mlp = (mlpin_s, mlpout_s)
+
+    def w_copy(i, source):
+        at = attnout_s.at[source, ring, core]
+        return remote(at, at, w_send.at[i], w_recv.at[source], tok, peer(i))
+
+    def mlp_copy(k):
+        return remote(
+            mlp[k].at[0, ring, core], mlp[k].at[1, ring, core], w_send.at[8 + k], w_recv.at[8 + k], tok, across
+        )
+
+    def spread_copy(k, step, place):
+        at = attnout_s.at[:, place, core] if k == 2 else mlp[k].at[1, place, core]
+        n = k * 3 + step - 1
+        return remote(at, at, v_send.at[n], v_recv.at[n], along_x(step), me)
+
+    def pair_copy(k, owner):
+        at = attnout_s.at[:, :, owner] if k == 2 else mlp[k].at[1, :, owner]
+        return remote(at, at, v_send.at[9 + k], v_recv.at[9 + k], sibling, me)
+
+    def spread_arrived(k):
+        for step in (1, 2, 3):
+            spread_copy(k, step, lax.rem(ring + 4 - step, 4)).wait_recv()
 
     lane = lane_of((SHARE, LANES))
 
-    def aggregate_step(i, carry):
-        field_copy(i).wait()
+    def p1_copy(i, source):
+        return remote(
+            part_s.at[i], part_r.at[source], p1_send.at[i], p1_recv.at[source], tok, peer(i)
+        )
+
+    def weigh(i):
+        at = i % 2
         for v in range(LOCAL_VARS):
-            emb_s[v * SHARE : (v + 1) * SHARE, :] = field_s[i, v] + own_embed[v : v + 1, :]
-        scores = mm_nt(emb_s[...], kq_s[...]).reshape(LOCAL_VARS, SHARE, LANES)
+            emb_s[at, v * SHARE : (v + 1) * SHARE, :] = field_s[i, v] + own_embed[v : v + 1, :]
+        scores = mm(emb_s[at], kq_s[...]).reshape(LOCAL_VARS, SHARE, LANES)
         highest = jnp.max(scores, axis=0)
         expd = jnp.exp(scores - highest[None])
         totals = jnp.sum(expd, axis=0)
         coarse = expd.astype(BF).astype(F32)
         weights = jnp.where((lane < 16)[None], coarse, jnp.where((lane < 32)[None], expd - coarse, 0.0))
-        weights = weights.reshape(LOCAL_VARS * SHARE, LANES).astype(BF)
-        for n in range(4):
-            cols = slice(n * 256, (n + 1) * 256)
-            wide = mm(weights, spread_s[:, cols])
-            projected = mm(emb_s[...], value_s[:, cols])
-            term = (wide * projected).reshape(LOCAL_VARS, SHARE, 256)
-            part_s[i, :, cols] = jnp.sum(term, axis=0).astype(BF)
+        weight_s[at] = weights.reshape(LOCAL_VARS * SHARE, LANES).astype(BF)
         high, middle, low = split_three(highest)
         high_t, middle_t, low_t = split_three(totals)
         notes = jnp.where(lane < 16, high, jnp.where(lane < 32, middle, low))
         notes_t = jnp.where(lane < 64, high_t, jnp.where(lane < 80, middle_t, low_t))
         part_s[i, :, WIDTH:] = jnp.where(lane < 48, notes, notes_t).astype(BF)
 
-        @pl.when(i < GROUPS - 1)
-        def _():
-            remote(
-                part_s.at[i], part_r.at[me], p1_send.at[i], p1_recv.at[me], tok, peer(i)
-            ).start()
-
-        return carry
-
-    lax.fori_loop(0, GROUPS, aggregate_step, 0)
+    def add_up(i):
+        at = i % 2
+        for n in range(2):
+            cols = slice(n * 512, (n + 1) * 512)
+            wide = mm(weight_s[at], spread_s[:, cols])
+            projected = mm(emb_s[at], value_s[:, cols])
+            term = (wide * projected).reshape(LOCAL_VARS, SHARE, 512)
+            part_s[i, :, cols] = jnp.sum(term, axis=0).astype(BF)
+
+    field_copy(0).wait()
+    weigh(0)
+    loads[3].wait()
+    for i in range(GROUPS):
+        if i + 2 < GROUPS:
+            field_copy(i + 2).start()
+        if i == 1:
+            for k in (4, 5, 6, 7):
+                loads[k].start()
+        if i == 4:
+            for k in (9, 10, 11):
+                loads[k].start()
+        if i + 1 < GROUPS:
+            field_copy(i + 1).wait()
+            weigh(i + 1)
+        add_up(i)
+        if i == 2:
+            pl.semaphore_wait(barrier, len(others))
+            for k in range(3):
+                p1_copy(k, me).start()
+        elif 2 < i < GROUPS - 1:
+            p1_copy(i, me).start()
+    loads[8].wait()
+    for i in range(GROUPS - 1):
+        w_copy(i, me).start()
     part_r[me] = part_s[GROUPS - 1]
-
-    def p1_copy(i):
-        return remote(
-            part_s.at[i], part_r.at[peer(i)], p1_send.at[i], p1_recv.at[peer(i)], tok, peer(i)
-        )
-
-    for i in range(GROUPS - 1):
-        p1_copy(i).wait_recv()
+    for i in range(GROUPS - 1):
+        p1_copy(i, peer(i)).wait_recv()
 
     notes = part_r[:, :, WIDTH:].reshape(ROWS, LANES)
     highest = mm(notes, pick_s[0]).reshape(GROUPS, SHARE, LANES)
@@ -273,7 +322,10 @@
     for i in range(GROUPS - 1):
         gather_copy(norm_r, p3_send, p3_recv, i, me).start()
     loads[7].wait()
-    loads[8].wait()
+    for i in range(GROUPS - 1):
+        w_copy(i, peer(i)).wait_recv()
+    for step in (1, 2, 3):
+        spread_copy(2, step, ring).start()
     for i in range(GROUPS - 1):
         gather_copy(norm_r, p3_send, p3_recv, i, peer(i)).wait_recv()
 
@@ -320,16 +372,13 @@
     ).astype(BF)
     z_q = remote(qout_s, qin_r, z_send.at[1], z_recv.at[0], partner, me)
     z_q.start()
-
-    w_rows = pl.ds(pl.multiple_of(core * 64, 64), 64)
-
-    def w_copy(i, source):
-        at = attnout_s.at[source, w_rows, :]
-        return remote(at, at, w_send.at[i], w_recv.at[source], tok, peer(i))
-
-    for i in range(GROUPS - 1):
-        w_copy(i, me).start()
-
+    for k in (10, 11):
+        loads[k].wait()
+    for k in range(2):
+        mlp_copy(k).start()
+
+    spread_arrived(2)
+    pair_copy(2, core).start()
     max_s[...] = jnp.full(max_s.shape, -jnp.inf, F32)
     acc_s[...] = jnp.zeros(acc_s.shape, F32)
     z_kv.wait_recv()
@@ -342,36 +391,46 @@
         left[: ROWS // 2], pltpu.roll(packed, 64, 1), 0.0
     ).astype(BF)
 
-    def absorb(at):
-        block = kv_r[at]
-        ones = jnp.where(left, 1.0, block.astype(F32)).astype(BF)
-        for n in range(3):
-            rows = slice(n * 256, (n + 1) * 256)
-            logits = mm_nt(q_s[rows, :], block)
-            before = max_s[rows, :]
-            newest = jnp.maximum(before, jnp.max(logits, axis=1, keepdims=True))
-            probs = jnp.exp(logits - jnp.concatenate([newest] * 3, axis=1)).astype(BF)
-            acc_s[rows, :] = acc_s[rows, :] * jnp.exp(before - newest) + mm(probs, ones)
-            max_s[rows, :] = newest
-
-    def attend_step(order, carry):
-        own = slot(order, core)
-        theirs = slot(order, 1 - core)
-
-        @pl.when(order > 1)
+    def pass_on(order):
+        share_copy(order, core).wait_recv()
+        share_copy(order, core).start()
+
+    share_copy(1, core).start()
+    pass_on(2)
+    pass_on(3)
+    many_left = lane_of((4 * ROWS, LANES)) < 64
+
+    def attend_step(step, carry):
+        @pl.when(step == 1)
         def _():
-            remote(kv_r.at[own], kv_r.at[own], kv_send.at[0], kv_recv.at[own], sibling, me).wait_recv()
-
-        @pl.when(order > 0)
+            pass_on(4)
+
+        @pl.when(step == 2)
         def _():
-            share_copy(order, core).start()
-
-        absorb(own)
-        share_copy(order, 1 - core).wait_recv()
-        absorb(theirs)
+            pass_on(5)
+            pass_on(6)
+
+        @pl.when(step == 3)
+        def _():
+            pass_on(7)
+            for k in range(2):
+                mlp_copy(k).wait_recv()
+                for hop in (1, 2, 3):
+                    spread_copy(k, hop, ring).start()
+
+        for order in (2 * step, 2 * step + 1):
+            share_copy(order, 1 - core).wait_recv()
+        block = kv_r[pl.ds(step * 4, 4)].reshape(4 * ROWS, LANES)
+        ones = jnp.where(many_left, 1.0, block.astype(F32)).astype(BF)
+        logits = mm_nt(q_s[...], block)
+        before = max_s[...]
+        newest = jnp.maximum(before, jnp.max(logits, axis=1, keepdims=True))
+        probs = jnp.exp(logits - jnp.concatenate([newest] * 12, axis=1)).astype(BF)
+        acc_s[...] = acc_s[...] * jnp.exp(before - newest) + mm(probs, ones)
+        max_s[...] = newest
         return carry
 
-    lax.fori_loop(0, 8, attend_step, 0)
+    lax.fori_loop(0, 4, attend_step, 0)
 
     acc = acc_s[...]
     turned = pltpu.roll(acc, 64, 1)
@@ -382,7 +441,7 @@
     att_r[half, me] = att_s[0, me]
 
     def att_copy(side, i, at, source):
-        to = lax.rem(me + 1 + i, GROUPS)
+        to = peer(i)
         return remote(
             att_s.at[side, to],
             att_r.at[at, source],
@@ -397,37 +456,52 @@
         att_copy(1, i, half, me).start()
     att_copy(1, GROUPS - 1, half, me).start()
 
-    def w_share(i, rows):
-        at = attnout_s.at[peer(i), rows, :]
-        return remote(at, at, w_send.at[GROUPS + i], w_recv.at[GROUPS + peer(i)], sibling, me)
-
-    their_rows = pl.ds(pl.multiple_of(64 - core * 64, 64), 64)
-    for i in range(GROUPS - 1):
-        w_copy(i, peer(i)).wait_recv()
-        w_share(i, w_rows).start()
-    for i in range(GROUPS - 1):
-        w_share(i, their_rows).wait_recv()
     for i in range(GROUPS - 1):
         att_copy(0, i, half, peer(i)).wait_recv()
     for i in range(GROUPS):
         att_copy(1, i, 1 - half, peer(i)).wait_recv()
 
+    pair_copy(2, 1 - core).wait_recv()
     attended = jnp.concatenate([att_r[0, g] + att_r[1, g] for g in range(GROUPS)], axis=1)
     attn_sum = mm(attended, attnout_s[...].reshape(WIDTH, WIDTH))
-    upd_r[me] = (stream.astype(F32) + attn_sum).astype(BF)
-    for i in range(GROUPS - 1):
-        gather_copy(upd_r, p8_send, p8_recv, i, me).start()
-    for k in (9, 10, 11):
-        loads[k].wait()
-    for i in range(GROUPS - 1):
-        gather_copy(upd_r, p8_send, p8_recv, i, peer(i)).wait_recv()
-
-    updated = upd_r[...].reshape(ROWS, WIDTH)
+    def along_y(i):
+        return lax.rem(high_y + 1 + i, 4)
+
+    def upd_copy(i, source):
+        at = upd_r.at[source]
+        return remote(at, at, p8_send.at[i], p8_recv.at[source], tok, plane * 4 + along_y(i))
+
+    def res_copy(i, source):
+        to = (1 - plane) * 4 + i
+        cols = pl.ds(pl.multiple_of(to * LANES, LANES), LANES)
+        return remote(
+            upd_r.at[high_y, :, cols], res_r.at[source], p8_send.at[4 + i], p8_recv.at[4 + source], tok, to
+        )
+
+    upd_r[high_y] = (stream.astype(F32) + attn_sum).astype(BF)
+    for i in range(3):
+        upd_copy(i, high_y).start()
+    for i in range(4):
+        res_copy(i, high_y).start()
+    loads[9].wait()
+    for k in range(2):
+        spread_arrived(k)
+        pair_copy(k, core).start()
+    for i in range(3):
+        upd_copy(i, along_y(i)).wait_recv()
+
+    updated = upd_r[...].reshape(ROWS // 2, WIDTH)
     normed_two = layer_norm(updated.astype(F32), gain2_s[...])
-    raised = mm(normed_two, mlpin_s[...])
-    hidden = (0.5 * raised * (1.0 + lax.erf(raised * 0.7071067811865476))).astype(BF)
+    for k in range(2):
+        pair_copy(k, 1 - core).wait_recv()
+    hidden = []
+    for k in range(2):
+        raised = mm(normed_two, mlpin_s[k].reshape(WIDTH, 512))
+        hidden.append((0.5 * raised * (1.0 + lax.erf(raised * 0.7071067811865476))).astype(BF))
+    hidden = jnp.concatenate(hidden, axis=1)
+    down_weight = mlpout_s[...].reshape(WIDTH, WIDTH)
     for n in range(4):
-        terms = mm(hidden, mlpout_s[:, n * 256 : (n + 1) * 256]).astype(BF)
+        terms = mm(hidden, down_weight[:, n * 256 : (n + 1) * 256]).astype(BF)
         down_s[2 * n] = terms[:, :LANES]
         down_s[2 * n + 1] = terms[:, LANES:]
 
@@ -443,21 +517,26 @@
 
     for i in range(GROUPS - 1):
         down_copy(i, me).start()
-    total = down_s[me].astype(F32)
+    down_r[me] = down_s[me]
     own_cols = pl.ds(pl.multiple_of(me * LANES, LANES), LANES)
-    residual = upd_r[:, :, own_cols].reshape(ROWS, LANES).astype(F32)
+    for i in range(4):
+        res_copy(i, i).wait_recv()
     for i in range(GROUPS - 1):
         down_copy(i, peer(i)).wait_recv()
-        total = total + down_r[peer(i)].astype(F32)
-    out[...] = (residual + total).astype(BF)
-
-    for i in range(GROUPS - 1):
-        p1_copy(i).wait_send()
+
+    def finish_half(which, residual):
+        terms = jnp.sum(down_r[pl.ds(which * 4, 4)].astype(F32), axis=0)
+        rows = pl.ds(pl.multiple_of(which * (ROWS // 2), 16), ROWS // 2)
+        out[rows, :] = (residual.reshape(ROWS // 2, LANES).astype(F32) + terms).astype(BF)
+
+    finish_half(plane, upd_r[:, :, own_cols])
+    finish_half(1 - plane, res_r[...])
+
+    for i in range(GROUPS - 1):
+        p1_copy(i, me).wait_send()
         gather_copy(norm_r, p3_send, p3_recv, i, me).wait_send()
         w_copy(i, me).wait_send()
-        w_share(i, w_rows).wait_send()
         att_copy(0, i, half, me).wait_send()
-        gather_copy(upd_r, p8_send, p8_recv, i, me).wait_send()
         down_copy(i, me).wait_send()
     for i in range(GROUPS):
         att_copy(1, i, half, me).wait_send()
@@ -467,6 +546,15 @@
         x_copy(3 + k, hops[k][0] + 3, slot(1, core)).wait_send()
     z_kv.wait_send()
     z_q.wait_send()
+    for i in range(3):
+        upd_copy(i, high_y).wait_send()
+        pair_copy(i, core).wait_send()
+        for step in (1, 2, 3):
+            spread_copy(i, step, ring).wait_send()
+    for i in range(4):
+        res_copy(i, high_y).wait_send()
+    for k in range(2):
+        mlp_copy(k).wait_send()
 
 
 def scratch():
@@ -482,14 +570,15 @@
         vmem((WIDTH, WIDTH), BF),
         vmem((1, WIDTH), F32),
         vmem((3, WIDTH, LANES), BF),
-        vmem((GROUPS, LANES, WIDTH), BF),
+        vmem((GROUPS, 4, 2, 16, WIDTH), BF),
         vmem((1, WIDTH), F32),
-        vmem((WIDTH, 512), BF),
-        vmem((512, WIDTH), BF),
-        vmem((LANES, WIDTH), BF),
+        vmem((2, 4, 2, LANES, 512), BF),
+        vmem((2, 4, 2, 64, WIDTH), BF),
+        vmem((WIDTH, LANES), BF),
         vmem((LANES, WIDTH), BF),
         vmem((2, LANES, LANES), BF),
-        vmem((LOCAL_VARS * SHARE, WIDTH), BF),
+        vmem((2, LOCAL_VARS * SHARE, WIDTH), BF),
+        vmem((2, LOCAL_VARS * SHARE, LANES), BF),
         vmem((GROUPS, SHARE, WIDTH + LANES), BF),
         vmem((GROUPS, SHARE, WIDTH + LANES), BF),
         vmem((GROUPS, SHARE, WIDTH), BF),
@@ -502,9 +591,10 @@
         vmem((2 * ROWS, LANES), F32),
         vmem((2, GROUPS, SHARE, LANES), BF),
         vmem((2, GROUPS, SHARE, LANES), BF),
-        vmem((GROUPS, SHARE, WIDTH), BF),
-        vmem((GROUPS, ROWS, LANES), BF),
-        vmem((GROUPS, ROWS, LANES), BF),
+        vmem((4, SHARE, WIDTH), BF),
+        vmem((4, SHARE, LANES), BF),
+        vmem((GROUPS, ROWS // 2, LANES), BF),
+        vmem((GROUPS, ROWS // 2, LANES), BF),
         dma((LOADS,)),
         dma((GROUPS,)),
         dma((GROUPS,)),
@@ -515,6 +605,8 @@
         dma((1,)),
         dma((16,)),
         dma((16,)),
+        dma((12,)),
+        dma((12,)),
         dma((2 * GROUPS,)),
         dma((2 * GROUPS,)),
         dma((2 * GROUPS,)),
@@ -560,10 +652,10 @@
         agg_out,
         gain_one.reshape(1, WIDTH),
         qkv_weight,
-        attn_out,
+        attn_out.reshape(4, 2, 16, WIDTH),
         gain_two.reshape(1, WIDTH),
-        mlp_in,
-        mlp_out,
+        mlp_in.reshape(4, 2, LANES, 512),
+        mlp_out.reshape(4, 2, 64, WIDTH),
     )
 
 

time: 101 us -> 79.9 us (0.79)
  Pallas kernels: 99.2 us -> 77.2 us
    pallas_call x1, Pallas kernels: 99.2 us -> 77.2 us  [body(): pl.pallas_call(kernel, out_shape=jax.ShapeDtypeStruct((ROWS, LANES), BF),...]
where the time goes in v2:
time: 79.9 us; the launch traced here: 78.8 us
  Pallas kernels  77.2 us (97%)
  local copies, waits for them, and re-layouts  1.54 us (2%)
    pallas_call x1, Pallas kernels, body(): pl.pallas_call(kernel, out_shape=jax.ShapeDtypeStruct((ROWS, LANES), BF),...  77.2 us

profile of v2, /device:TPU:0, one launch (start us, length us, event | category | flops | bytes accessed | tf_op | source)
XLA Modules:
  0.0 78.8 jit_solution(8496345219645806383)
XLA Ops:
  0.0 77.2 %shard_map.127 = bf16[384,128]{1,0:T(8,128)(2,1)} custom-call(bf16[6,384,1024]{2,1,0:T(8,128)(2,1)} %fields.1, bf16[48,1024]{1,0:T(8,128)(2,1)} %var_embed.1, bf16[384,1024]{1,0:T(8,128)(2,1)} %pos_embed.1, bf16[1024,1024]{1,0:T(8,128)(2,1)} %agg_key.1, f32[16,64]{1,0:T(8,128)} %agg_query.1, bf16[1024,1024]{1,0:T(8,128)(2,1)} %agg_value.1, ...), custom_call_target="tpu_custom_call" | custom-call | tf_op jit(solution)/shard_map/pallas_call | solution.py:636
  77.2 1.5 %copy.15 = bf16[384,128]{1,0:T(8,128)(2,1)} copy(bf16[384,128]{1,0:T(8,128)(2,1)} %shard_map.127) | data formatting | bytes 196608

commit v3 on v2

--- a/solution.py
+++ b/solution.py
@@ -284,11 +284,9 @@
             field_copy(i + 1).wait()
             weigh(i + 1)
         add_up(i)
-        if i == 2:
+        if i == 0:
             pl.semaphore_wait(barrier, len(others))
-            for k in range(3):
-                p1_copy(k, me).start()
-        elif 2 < i < GROUPS - 1:
+        if i < GROUPS - 1:
             p1_copy(i, me).start()
     loads[8].wait()
     for i in range(GROUPS - 1):

time: 79.9 us -> 78.6 us (0.984)
  Pallas kernels: 77.2 us -> 76 us
    pallas_call x1, Pallas kernels: 77.2 us -> 76 us  [body(): pl.pallas_call(kernel, out_shape=jax.ShapeDtypeStruct((ROWS, LANES), BF),...]
where the time goes in v3:
time: 78.6 us; the launch traced here: 77.5 us
  Pallas kernels  76 us (97%)
  local copies, waits for them, and re-layouts  1.54 us (2%)
    pallas_call x1, Pallas kernels, body(): pl.pallas_call(kernel, out_shape=jax.ShapeDtypeStruct((ROWS, LANES), BF),...  76 us

profile of v3, /device:TPU:0, one launch (start us, length us, event | category | flops | bytes accessed | tf_op | source)
XLA Modules:
  0.0 77.5 jit_solution(16070749784698000883)
XLA Ops:
  0.0 76.0 %shard_map.127 = bf16[384,128]{1,0:T(8,128)(2,1)} custom-call(bf16[6,384,1024]{2,1,0:T(8,128)(2,1)} %fields.1, bf16[48,1024]{1,0:T(8,128)(2,1)} %var_embed.1, bf16[384,1024]{1,0:T(8,128)(2,1)} %pos_embed.1, bf16[1024,1024]{1,0:T(8,128)(2,1)} %agg_key.1, f32[16,64]{1,0:T(8,128)} %agg_query.1, bf16[1024,1024]{1,0:T(8,128)(2,1)} %agg_value.1, ...), custom_call_target="tpu_custom_call" | custom-call | tf_op jit(solution)/shard_map/pallas_call | solution.py:634
  76.0 1.5 %copy.15 = bf16[384,128]{1,0:T(8,128)(2,1)} copy(bf16[384,128]{1,0:T(8,128)(2,1)} %shard_map.127) | data formatting | bytes 196608

commit v4 on v3

--- a/solution.py
+++ b/solution.py
@@ -319,6 +319,10 @@
 
     for i in range(GROUPS - 1):
         gather_copy(norm_r, p3_send, p3_recv, i, me).start()
+    for k in (10, 11):
+        loads[k].wait()
+    for k in range(2):
+        mlp_copy(k).start()
     loads[7].wait()
     for i in range(GROUPS - 1):
         w_copy(i, peer(i)).wait_recv()
@@ -370,10 +374,6 @@
     ).astype(BF)
     z_q = remote(qout_s, qin_r, z_send.at[1], z_recv.at[0], partner, me)
     z_q.start()
-    for k in (10, 11):
-        loads[k].wait()
-    for k in range(2):
-        mlp_copy(k).start()
 
     spread_arrived(2)
     pair_copy(2, core).start()
@@ -405,16 +405,16 @@
 
         @pl.when(step == 2)
         def _():
-            pass_on(5)
-            pass_on(6)
-
-        @pl.when(step == 3)
-        def _():
-            pass_on(7)
             for k in range(2):
                 mlp_copy(k).wait_recv()
                 for hop in (1, 2, 3):
                     spread_copy(k, hop, ring).start()
+            pass_on(5)
+            pass_on(6)
+
+        @pl.when(step == 3)
+        def _():
+            pass_on(7)
 
         for order in (2 * step, 2 * step + 1):
             share_copy(order, 1 - core).wait_recv()

time: 78.6 us -> 76.6 us (0.975); the launches traced: 77.5 us -> 76.4 us
  Pallas kernels: 76 us -> 74.8 us
    pallas_call x1, Pallas kernels: 76 us -> 74.8 us  [body(): pl.pallas_call(kernel, out_shape=jax.ShapeDtypeStruct((ROWS, LANES), BF),...]
where the time goes in v4:
time: 76.6 us; the launch traced here: 76.4 us
  Pallas kernels  74.8 us (98%)
  local copies, waits for them, and re-layouts  1.54 us (2%)
    pallas_call x1, Pallas kernels, body(): pl.pallas_call(kernel, out_shape=jax.ShapeDtypeStruct((ROWS, LANES), BF),...  74.8 us
    unnamed x1, local copies, waits for them, and re-layouts  1.54 us

profile of v4, /device:TPU:0, one launch (start us, length us, event | category | flops | bytes accessed | tf_op | source)
XLA Modules:
  0.0 76.4 jit_solution(3480923828643224086)
XLA Ops:
  0.0 74.8 %shard_map.127 = bf16[384,128]{1,0:T(8,128)(2,1)} custom-call(bf16[6,384,1024]{2,1,0:T(8,128)(2,1)} %fields.1, bf16[48,1024]{1,0:T(8,128)(2,1)} %var_embed.1, bf16[384,1024]{1,0:T(8,128)(2,1)} %pos_embed.1, bf16[1024,1024]{1,0:T(8,128)(2,1)} %agg_key.1, f32[16,64]{1,0:T(8,128)} %agg_query.1, bf16[1024,1024]{1,0:T(8,128)(2,1)} %agg_value.1, ...), custom_call_target="tpu_custom_call" | custom-call | tf_op jit(solution)/shard_map/pallas_call | solution.py:634
  74.8 1.5 %copy.15 = bf16[384,128]{1,0:T(8,128)(2,1)} copy(bf16[384,128]{1,0:T(8,128)(2,1)} %shard_map.127) | data formatting | bytes 196608

commit v5 on v4

--- a/solution.py
+++ b/solution.py
@@ -402,13 +402,13 @@
         @pl.when(step == 1)
         def _():
             pass_on(4)
-
-        @pl.when(step == 2)
-        def _():
             for k in range(2):
                 mlp_copy(k).wait_recv()
                 for hop in (1, 2, 3):
                     spread_copy(k, hop, ring).start()
+
+        @pl.when(step == 2)
+        def _():
             pass_on(5)
             pass_on(6)
 

time: 76.6 us -> 76.6 us (level)
  no operation moved by 1% of the time
where the time goes in v5:
time: 76.6 us; the launch traced here: 76.4 us
  Pallas kernels  74.8 us (98%)
  local copies, waits for them, and re-layouts  1.54 us (2%)
    pallas_call x1, Pallas kernels, body(): pl.pallas_call(kernel, out_shape=jax.ShapeDtypeStruct((ROWS, LANES), BF),...  74.8 us
    unnamed x1, local copies, waits for them, and re-layouts  1.54 us

profile of v5, /device:TPU:0, one launch (start us, length us, event | category | flops | bytes accessed | tf_op | source)
XLA Modules:
  0.0 76.4 jit_solution(8995592171552526370)
XLA Ops:
  0.0 74.8 %shard_map.127 = bf16[384,128]{1,0:T(8,128)(2,1)} custom-call(bf16[6,384,1024]{2,1,0:T(8,128)(2,1)} %fields.1, bf16[48,1024]{1,0:T(8,128)(2,1)} %var_embed.1, bf16[384,1024]{1,0:T(8,128)(2,1)} %pos_embed.1, bf16[1024,1024]{1,0:T(8,128)(2,1)} %agg_key.1, f32[16,64]{1,0:T(8,128)} %agg_query.1, bf16[1024,1024]{1,0:T(8,128)(2,1)} %agg_value.1, ...), custom_call_target="tpu_custom_call" | custom-call | tf_op jit(solution)/shard_map/pallas_call | solution.py:634
  74.8 1.5 %copy.15 = bf16[384,128]{1,0:T(8,128)(2,1)} copy(bf16[384,128]{1,0:T(8,128)(2,1)} %shard_map.127) | data formatting | bytes 196608
